TPU v7x, 128 devices: a whole 4x4x4 slice. The times are simulated.
128 devices in a mesh: grp: 8 (over x, y_hi), seq: 16 (over y_lo, z, core).
Axes of the slice: x: 4, y: 4 (y_hi: 2, y_lo: 2; y = y_hi * 2 + y_lo), z: 4, core: 2. Of those that a mesh axis runs over, the one named last changes fastest.
Arguments:
- queries: bfloat16 [32768, 4096], P(('grp', 'seq')), parts along dimension 0, may hold values from -200 to 200
- keys_resp: bfloat16 [32768, 512], P(('grp', 'seq')), parts along dimension 0, may hold values from -6 to 6
- values_resp: bfloat16 [32768, 512], P(('grp', 'seq')), parts along dimension 0, may hold values from -12 to 12
- keys_prompt: bfloat16 [8192, 512], P(('grp', 'seq')), parts along dimension 0, may hold values from -6 to 6
- values_prompt: bfloat16 [8192, 512], P(('grp', 'seq')), parts along dimension 0, may hold values from -12 to 12
- grad_out: bfloat16 [32768, 4096], P(('grp', 'seq')), parts along dimension 0, may hold values from -48 to 48
- resp_len: int32 [128], P(('grp', 'seq')), parts along dimension 0, may hold values from 128 to 256, as said below
Outputs:
- grad_queries: bfloat16 [32768, 4096], P(('grp', 'seq')), parts along dimension 0
- grad_keys_resp: bfloat16 [32768, 512], P(('grp', 'seq')), parts along dimension 0
- grad_values_resp: bfloat16 [32768, 512], P(('grp', 'seq')), parts along dimension 0
- grad_keys_prompt: bfloat16 [8192, 512], P(('grp', 'seq')), parts along dimension 0
- grad_values_prompt: bfloat16 [8192, 512], P(('grp', 'seq')), parts along dimension 0
There are 8 independent parts, one for each index of `grp`. A program takes and returns all parts, laid end to end along the dimension named above; each array names one. Nothing has to cross between parts.
Inputs may be any that keep to these rules, and one draw needn't show every extreme that they name: `resp_len`: each length is a multiple of 128; in every group some rollout has length 256.
All inputs are finite; a program needn't handle non-finite values.
Results may differ from a plain program's by a relative error of at most 0.022.
Values may be sent and summed in bfloat16 or wider, within the bound.
A program may use at most 128 MiB of HBM per device.

v0:
```python
import jax
import jax.numpy as jnp
from jax import lax
from jax.sharding import PartitionSpec as P

HEAD_SIZE = 128


def row_block(query_rows, grad_rows, all_keys, all_values, prompt_n, from_key):
    num_rows = query_rows.shape[0]
    key_span = all_keys.shape[0]
    width_kv = all_keys.shape[1]
    heads_kv = width_kv // HEAD_SIZE
    group_width = query_rows.shape[1] // heads_kv
    groups = group_width // HEAD_SIZE
    att_scale = HEAD_SIZE ** (-0.5)
    key_pos = lax.broadcasted_iota(jnp.int32, (num_rows, key_span), 1)
    query_pos = lax.broadcasted_iota(jnp.int32, (num_rows, key_span), 0)
    visible = (key_pos < prompt_n) | (key_pos - prompt_n <= query_pos)

    def per_head(head_idx, state_tuple):
        grad_query, key_sums, value_sums, log_totals, deltas_all = state_tuple
        query_head = lax.dynamic_slice_in_dim(
            query_rows, head_idx * group_width, group_width, 1
        ).reshape(num_rows, groups, HEAD_SIZE)
        grad_head = lax.dynamic_slice_in_dim(
            grad_rows, head_idx * group_width, group_width, 1
        ).reshape(num_rows, groups, HEAD_SIZE)
        key_head = lax.dynamic_slice_in_dim(all_keys, head_idx * HEAD_SIZE, HEAD_SIZE, 1)
        value_head = lax.dynamic_slice_in_dim(all_values, head_idx * HEAD_SIZE, HEAD_SIZE, 1)
        scores = (
            jnp.einsum("rgd,ld->grl", query_head, key_head, preferred_element_type=jnp.float32)
            * att_scale
        )
        scores = jnp.where(visible[None], scores, -jnp.inf)
        row_max = jnp.max(scores, axis=-1)
        log_total = row_max + jnp.log(jnp.sum(jnp.exp(scores - row_max[..., None]), axis=-1))
        probs = jnp.exp(scores - log_total[..., None])
        grad_probs = jnp.einsum(
            "rgd,ld->grl", grad_head, value_head, preferred_element_type=jnp.float32
        )
        deltas = jnp.sum(probs * grad_probs, axis=-1)
        grad_scores = probs * (grad_probs - deltas[..., None])
        probs_low = probs.astype(jnp.bfloat16)
        scores_low = grad_scores.astype(jnp.bfloat16)
        query_term = (
            jnp.einsum("grl,ld->rgd", scores_low, key_head, preferred_element_type=jnp.float32)
            * att_scale
        )
        query_term = query_term.reshape(num_rows, group_width).astype(jnp.bfloat16)
        key_term = (
            jnp.einsum("grl,rgd->ld", scores_low, query_head, preferred_element_type=jnp.float32)
            * att_scale
        )
        value_term = jnp.einsum(
            "grl,rgd->ld", probs_low, grad_head, preferred_element_type=jnp.float32
        )
        grad_query = lax.dynamic_update_slice_in_dim(
            grad_query, query_term, head_idx * group_width, 1
        )
        key_sums = lax.dynamic_update_slice_in_dim(key_sums, key_term, head_idx * HEAD_SIZE, 1)
        value_sums = lax.dynamic_update_slice_in_dim(
            value_sums, value_term, head_idx * HEAD_SIZE, 1
        )
        log_totals = lax.dynamic_update_slice_in_dim(log_totals, log_total, head_idx * groups, 0)
        deltas_all = lax.dynamic_update_slice_in_dim(deltas_all, deltas, head_idx * groups, 0)
        return (grad_query, key_sums, value_sums, log_totals, deltas_all)

    initial = (
        jnp.zeros(query_rows.shape, jnp.bfloat16),
        jnp.zeros((key_span - from_key, width_kv), jnp.float32),
        jnp.zeros((key_span - from_key, width_kv), jnp.float32),
        jnp.zeros((heads_kv * groups, num_rows), jnp.float32),
        jnp.zeros((heads_kv * groups, num_rows), jnp.float32),
    )
    return lax.fori_loop(0, heads_kv, per_head, initial)


def shards(queries, keys_resp, values_resp, keys_prompt, values_prompt, grad_out, resp_len):
    gathered_k, gathered_v = (
        lax.all_gather(keys_prompt, "seq", axis=0, tiled=True),
        lax.all_gather(values_prompt, "seq", axis=0, tiled=True),
    )
    prompt_n = gathered_k.shape[0]
    resp_rows = queries.shape[0]
    all_keys = jnp.concatenate([gathered_k, keys_resp], 0)
    all_values = jnp.concatenate([gathered_v, values_resp], 0)
    length = resp_len[0]
    is_live = lax.broadcasted_iota(jnp.int32, (resp_rows, 1), 0) < length
    masked = jnp.where(is_live, grad_out, jnp.zeros_like(grad_out))
    from_key = 0
    grad_query, key_sums, value_sums, log_totals, deltas_all = row_block(
        queries, masked, all_keys, all_values, prompt_n, from_key
    )
    grad_keys_resp = key_sums[prompt_n:].astype(jnp.bfloat16)
    grad_values_resp = value_sums[prompt_n:].astype(jnp.bfloat16)
    prompt_keys_grad, prompt_values_grad = (
        lax.psum_scatter(
            key_sums[:prompt_n].astype(jnp.bfloat16), "seq", scatter_dimension=0, tiled=True
        ).astype(jnp.float32),
        lax.psum_scatter(
            value_sums[:prompt_n].astype(jnp.bfloat16), "seq", scatter_dimension=0, tiled=True
        ).astype(jnp.float32),
    )
    return (
        grad_query,
        grad_keys_resp,
        grad_values_resp,
        prompt_keys_grad.astype(jnp.bfloat16),
        prompt_values_grad.astype(jnp.bfloat16),
    )


def solution(mesh):
    placed = (
        P(("grp", "seq"), None),
        P(("grp", "seq"), None),
        P(("grp", "seq"), None),
        P(("grp", "seq"), None),
        P(("grp", "seq"), None),
        P(("grp", "seq"), None),
        P(("grp", "seq")),
    )
    return jax.shard_map(
        shards,
        mesh=mesh,
        in_specs=placed,
        out_specs=(
            P(("grp", "seq"), None),
            P(("grp", "seq"), None),
            P(("grp", "seq"), None),
            P(("grp", "seq"), None),
            P(("grp", "seq"), None),
        ),
        check_vma=False,
    )
```

profile of v0, /device:TPU:1, one launch (start us, length us, event | category | flops | bytes accessed | tf_op | source)
XLA Modules:
  0.0 289.8 jit_solution(11887460992106838979)
XLA Ops:
  9.3 3.3 %copy.22 = bf16[256,4096]{0,1:T(8,128)(2,1)S(1)} copy(bf16[256,4096]{1,0:T(8,128)(2,1)} %param.14) | data formatting | bytes 4194304 | tf_op args[5]
  12.7 1.5 broadcast_select_fusion
  14.2 31.8 %all-gather.5.cloned.1.call-done = bf16[1024,512]{1,0:T(8,128)(2,1)} async-done(((bf16[64,512]{1,0:T(8,128)(2,1)}), bf16[1024,512]{1,0:T(8,128)(2,1)}) %all-gather.5.cloned.1.call-update) | async-done | bytes 1048592 | tf_op jit(solution)/shard_map/all_gather | solution.py:82
  45.9 2.4 pad_maximum_fusion.1
  48.3 31.9 %all-gather.3.cloned.1.call-done = bf16[1024,512]{1,0:T(8,128)(2,1)} async-done(((bf16[64,512]{1,0:T(8,128)(2,1)}), bf16[1024,512]{1,0:T(8,128)(2,1)}) %all-gather.3.cloned.1.call-update) | async-done | bytes 1048592 | tf_op jit(solution)/shard_map/all_gather | solution.py:81
  80.2 1.3 pad_maximum_fusion
  81.5 1.2 broadcast.50.clone
  82.7 1.2 broadcast.50
  83.9 1.6 broadcast.49.clone
  85.4 75.2 %while.18 = (s32[]{:T(128)}, bf16[256,4096]{1,0:T(8,128)(2,1)}, bf16[1280,512]{1,0:T(8,128)(2,1)}, bf16[1280,512]{1,0:T(8,128)(2,1)}, bf16[1280,512]{1,0:T(8,128...) while((s32[]{:T(128)}, bf16[256,4096]{1,0:T(8,128)(2,1)}, ...), condition=%wide.region_4.5_spmd.clone, body=%wide.region_0.4_spmd.clone.sunk | while | flops 3393482752 | bytes 110525000 | solution.py:76
  86.3 1.1 constant_dynamic-slice_fusion.5
  87.4 1.1 constant_dynamic-slice_fusion.4
  88.7 1.6 fusion.60
  90.4 1.4 exponential_reduce_fusion.2
  91.7 2.3 fusion.65
  94.1 2.9 %fusion.61 = (f32[8,256]{1,0:T(8,128)S(1)}, f32[1280,256,8]{1,0,2:T(8,128)S(1)}) fusion(f32[8,256,1280]{1,2,0:T(8,128)S(1)} %get-tuple-element.297, f32[8,256]{1,0:T(8,128)S(1)} %log_add_fusion.2, bf16[256,8,128]{0,2,1:T(8,128)(2,1)S(1)} %bitcast.80, bf16[1280,512]{1,0:T(8,128)(2,1)} %get-tuple-element.339, s32[]{:T(128)S(6)} %select_n.40), kind=kOutput, calls=%fused_computation.3.clone.1 | convolution fusion | flops 678950912 | bytes 21839876 | tf_op jit(solution)/shard_map/while/body/eval_jaxpr/rgd,ld->grl/dot_general | solution.py:39
  97.0 2.1 fusion.62
  100.4 1.6 fusion.64
  102.1 1.1 copy-done.1
  105.1 1.1 constant_dynamic-slice_fusion.5
  106.2 1.1 constant_dynamic-slice_fusion.4
  107.5 1.6 fusion.60
  109.1 1.4 exponential_reduce_fusion.2
  110.5 2.3 fusion.65
  112.9 2.9 %fusion.61 = (f32[8,256]{1,0:T(8,128)S(1)}, f32[1280,256,8]{1,0,2:T(8,128)S(1)}) fusion(f32[8,256,1280]{1,2,0:T(8,128)S(1)} %get-tuple-element.297, f32[8,256]{1,0:T(8,128)S(1)} %log_add_fusion.2, bf16[256,8,128]{0,2,1:T(8,128)(2,1)S(1)} %bitcast.80, bf16[1280,512]{1,0:T(8,128)(2,1)} %get-tuple-element.339, s32[]{:T(128)S(6)} %select_n.40), kind=kOutput, calls=%fused_computation.3.clone.1 | convolution fusion | flops 678950912 | bytes 21839876 | tf_op jit(solution)/shard_map/while/body/eval_jaxpr/rgd,ld->grl/dot_general | solution.py:39
  115.8 2.1 fusion.62
  119.2 1.6 fusion.64
  123.9 1.1 constant_dynamic-slice_fusion.5
  125.0 1.1 constant_dynamic-slice_fusion.4
  126.3 1.7 fusion.60
  127.9 1.4 exponential_reduce_fusion.2
  129.3 2.3 fusion.65
  131.7 3.0 %fusion.61 = (f32[8,256]{1,0:T(8,128)S(1)}, f32[1280,256,8]{1,0,2:T(8,128)S(1)}) fusion(f32[8,256,1280]{1,2,0:T(8,128)S(1)} %get-tuple-element.297, f32[8,256]{1,0:T(8,128)S(1)} %log_add_fusion.2, bf16[256,8,128]{0,2,1:T(8,128)(2,1)S(1)} %bitcast.80, bf16[1280,512]{1,0:T(8,128)(2,1)} %get-tuple-element.339, s32[]{:T(128)S(6)} %select_n.40), kind=kOutput, calls=%fused_computation.3.clone.1 | convolution fusion | flops 678950912 | bytes 21839876 | tf_op jit(solution)/shard_map/while/body/eval_jaxpr/rgd,ld->grl/dot_general | solution.py:39
  134.6 2.1 fusion.62
  138.0 1.6 fusion.64
  142.7 1.1 constant_dynamic-slice_fusion.5
  143.8 1.1 constant_dynamic-slice_fusion.4
  145.1 1.7 fusion.60
  146.8 1.4 exponential_reduce_fusion.2
  148.2 2.3 fusion.65
  150.5 2.9 %fusion.61 = (f32[8,256]{1,0:T(8,128)S(1)}, f32[1280,256,8]{1,0,2:T(8,128)S(1)}) fusion(f32[8,256,1280]{1,2,0:T(8,128)S(1)} %get-tuple-element.297, f32[8,256]{1,0:T(8,128)S(1)} %log_add_fusion.2, bf16[256,8,128]{0,2,1:T(8,128)(2,1)S(1)} %bitcast.80, bf16[1280,512]{1,0:T(8,128)(2,1)} %get-tuple-element.339, s32[]{:T(128)S(6)} %select_n.40), kind=kOutput, calls=%fused_computation.3.clone.1 | convolution fusion | flops 678950912 | bytes 21839876 | tf_op jit(solution)/shard_map/while/body/eval_jaxpr/rgd,ld->grl/dot_general | solution.py:39
  153.4 2.1 fusion.62
  156.8 1.6 fusion.64
  160.6 2.4 slice.23
  163.1 1.1 slice.22
  164.2 1.7 slice.21
  166.6 54.0 %reduce-scatter.5.cloned.1.call-done = bf16[64,512]{1,0:T(8,128)(2,1)} async-done(((bf16[1024,512]{1,0:T(8,128)(2,1)}), bf16[64,512]{1,0:T(8,128)(2,1)}) %reduce-scatter.5.cloned.1.call-update) | async-done | bytes 65552 | tf_op jit(solution)/shard_map/reduce_scatter | solution.py:101
  220.6 62.7 %reduce-scatter.3.cloned.1.call-done = bf16[64,512]{1,0:T(8,128)(2,1)} async-done(((bf16[1024,512]{1,0:T(8,128)(2,1)}), bf16[64,512]{1,0:T(8,128)(2,1)}) %reduce-scatter.3.cloned.1.call-update) | async-done | bytes 65552 | tf_op jit(solution)/shard_map/reduce_scatter | solution.py:98
  (57 shorter events, 19.4 us)
Async XLA Ops:
  7.2 38.8 %all-gather.5.cloned.1.call-start = ((), (), s32[]{:S(2)}) async-start(), calls=%async_computation.3 | async-start | bytes 1114112 | tf_op jit(solution)/shard_map/all_gather | solution.py:82
  7.9 72.3 %all-gather.3.cloned.1.call-start = ((), (), s32[]{:S(2)}) async-start(), calls=%async_computation.2 | async-start | bytes 1114112 | tf_op jit(solution)/shard_map/all_gather | solution.py:81
  8.6 211.9 %reduce-scatter.5.cloned.1.call-start = ((), (), s32[]{:S(2)}) async-start(), calls=%async_computation.5 | async-start | bytes 1114112 | tf_op jit(solution)/shard_map/reduce_scatter | solution.py:101
  12.6 33.3 %copy-start.3 = (bf16[256,512]{1,0:T(8,128)(2,1)S(1)}, bf16[256,512]{1,0:T(8,128)(2,1)}, u32[]{:S(2)}) copy-start(bf16[256,512]{1,0:T(8,128)(2,1)} %param.11) | copy-start | bytes 786436
  12.7 67.5 %copy-start.4 = (bf16[256,512]{1,0:T(8,128)(2,1)S(1)}, bf16[256,512]{1,0:T(8,128)(2,1)}, u32[]{:S(2)}) copy-start(bf16[256,512]{1,0:T(8,128)(2,1)} %param.10) | copy-start | bytes 786436
  99.1 1.3 copy-start
  102.1 1.1 copy-start.1
  117.9 1.3 copy-start
  120.9 1.1 copy-start.1
  136.7 1.3 copy-start
  139.7 1.1 copy-start.1
  155.5 1.3 copy-start
  158.5 1.1 copy-start.1
  160.6 2.4 copy-start.2
  163.0 120.3 %reduce-scatter.3.cloned.1.call-start = ((), (), s32[]{:S(2)}) async-start(), calls=%async_computation.4 | async-start | bytes 1114112 | tf_op jit(solution)/shard_map/reduce_scatter | solution.py:98
Sparse Core Ops, SparseCore 0:
  9.7 36.1 all-gather.4
  47.6 32.4 all-gather.2
  163.1 57.4 reduce-scatter.4
  223.5 59.7 reduce-scatter.2
where the time goes:
time: 294 us; the launch traced here: 290 us
  waiting for transfers between devices  182 us (62%)
  matrix products  37.9 us (13%)
  local copies, waits for them, and re-layouts  32.5 us (11%)
  other arithmetic  22.6 us (8%)
  between operations  14.5 us (5%)
    reduce_scatter x1, waiting for transfers between devices, shards(): lax.psum_scatter(key_sums[:prompt_n].astype(jnp.bfloat16), 'seq', scatter...  62.7 us
    reduce_scatter x1, waiting for transfers between devices, shards(): lax.psum_scatter(value_sums[:prompt_n].astype(jnp.bfloat16), 'seq', scatt...  54 us
    all_gather x1, waiting for transfers between devices, shards(): lax.all_gather(keys_prompt, 'seq', axis=0, tiled=True)  31.9 us
    all_gather x1, waiting for transfers between devices, shards(): lax.all_gather(values_prompt, 'seq', axis=0, tiled=True)  31.8 us
    dot_general x4, matrix products, per_head(): jnp.einsum('rgd,ld->grl', grad_head, value_head, preferred_element_type=j...  11.8 us
    dot_general x4, matrix products, per_head(): jnp.einsum('grl,rgd->ld', probs_low, grad_head, preferred_element_type=jn...  9.35 us
    convert_element_type x4, other arithmetic, per_head(): scores_low = grad_scores.astype(jnp.bfloat16)  8.24 us
    dot_general x4, matrix products, per_head(): jnp.einsum('grl,rgd->ld', scores_low, query_head, preferred_element_type=...  6.59 us
  transfers between devices with their start and end apart: 4, of which 4 were waited for; matrix products, arithmetic and copies ran while one was open for 4% of the time, Pallas kernels for 0%

commit v1 on v0

v1 whole, which is shorter than its diff:
```python
import functools

import jax
import jax.numpy as jnp
from jax import lax
from jax.experimental import pallas as pl
from jax.experimental.pallas import tpu as pltpu
from jax.sharding import PartitionSpec as P

D = 128
HK = 4
G = 8
ROWS = 256
PROMPT = 1024
SPAN = PROMPT + ROWS
SHARD = 64
CHIPS = 8
HALF = CHIPS * SHARD
PAIRS = HK * G // 2
BLK = 256
W = 2 * ROWS
SCALE = D**-0.5
LOG2E = 1.4426950408889634
NEG = -1e30
BF = jnp.bfloat16
F32 = jnp.float32


def dot(a, b):
    return lax.dot_general(a, b, (((1,), (0,)), ((), ())), preferred_element_type=F32)


def fold(x, op):
    return op(x.reshape(x.shape[0] // 8, 8, x.shape[1]), axis=0)


def lanes(i, n=1):
    return pl.ds(pl.multiple_of(i * D, D), n * D)


def kernel(
    q_hbm, g_hbm, kr_hbm, vr_hbm, kp_hbm, vp_hbm, len_ref,
    dq_hbm, dkr_hbm, dvr_hbm, dkp_hbm, dvp_hbm,
    q_in, g_in, kv, s0, s1, d0, d1, p0, p1, mx, lx, dx, ms, ds_, rs, q_t, g_t, k_t, gs, qs,
    dq_acc, bias, acc, dq_out, part, sib, comb, land, fin_out,
    in_sem, own_sem, dq_sem, fin_sem, ag_send, ag_recv, rl_send, rl_recv, sx_send, sx_recv, sc_send, sc_recv,
):
    s_buf, d_buf, p_buf = [s0, s1], [d0, d1], [p0, p1]
    me = lax.axis_index("seq")
    core, chip = lax.rem(me, 2), me // 2
    sibling = me + 1 - 2 * core

    def peer(o):
        return 2 * lax.rem(chip + o, CHIPS) + core

    def remote(src, dst, send, recv, to):
        return pltpu.make_async_remote_copy(
            src_ref=src, dst_ref=dst, send_sem=send, recv_sem=recv,
            device_id={"seq": to}, device_id_type=pl.DeviceIdType.MESH,
        )

    own = pl.ds(pl.multiple_of(core * HALF + chip * SHARD, SHARD), SHARD)
    mine = pl.ds(pl.multiple_of(core * HALF, HALF), HALF)
    theirs = pl.ds(pl.multiple_of((1 - core) * HALF, HALF), HALF)

    own_copies = []
    for h in range(HK):
        for w, (p_hbm, r_hbm) in enumerate(((kp_hbm, kr_hbm), (vp_hbm, vr_hbm))):
            col = pl.ds(h * D, D)
            c = pltpu.make_async_copy(p_hbm.at[:, col], kv.at[h, w, own, :], own_sem.at[h, w, 0])
            c.start()
            r = pltpu.make_async_copy(r_hbm.at[:, col], kv.at[h, w, pl.ds(PROMPT, ROWS), :], own_sem.at[h, w, 1])
            r.start()
            own_copies.append((c, r))
    q_copy = pltpu.make_async_copy(q_hbm, q_in, in_sem.at[0])
    g_copy = pltpu.make_async_copy(g_hbm, g_in, in_sem.at[1])
    q_copy.start()
    g_copy.start()

    barrier = pltpu.get_barrier_semaphore()
    for o in range(1, CHIPS):
        pl.semaphore_signal(barrier, inc=1, device_id={"seq": peer(o)}, device_id_type=pl.DeviceIdType.MESH)
    pl.semaphore_signal(barrier, inc=1, device_id={"seq": sibling}, device_id_type=pl.DeviceIdType.MESH)
    pl.semaphore_wait(barrier, CHIPS)

    for h in range(HK):
        own_copies[2 * h][0].wait()
        own_copies[2 * h + 1][0].wait()
        blk = kv.at[h, :, own, :]
        for o in range(1, CHIPS):
            remote(blk, blk, ag_send.at[h], ag_recv.at[h], peer(o)).start()

    def seven(h):
        return kv.at[h, :, pl.ds(0, (CHIPS - 1) * SHARD), :]

    def relay(h):
        x = seven(h)
        pltpu.make_async_copy(x, x, ag_recv.at[h]).wait()
        y = kv.at[h, :, mine, :]
        remote(y, y, rl_send.at[h], rl_recv.at[h], sibling).start()

    def relayed(h):
        y = kv.at[h, :, theirs, :]
        remote(y, y, rl_send.at[h], rl_recv.at[h], sibling).wait_recv()

    def keys_ready(h):
        relayed(h)
        k_t[h] = kv[h, 0].T

    q_copy.wait()
    g_copy.wait()
    live = lax.broadcasted_iota(jnp.int32, (D, ROWS), 1) < len_ref[0]

    def prep(i, _):
        q_t[i] = q_in[:, lanes(i)].T
        gt = g_in[:, lanes(i)].T.astype(F32)
        g_t[i] = jnp.where(live, gt, 0.0).astype(BF)
        return 0

    lax.fori_loop(0, HK * G, prep, 0)
    acc[...] = jnp.zeros(acc.shape, F32)
    key = lax.broadcasted_iota(jnp.int32, (BLK, ROWS), 0)
    row = lax.broadcasted_iota(jnp.int32, (BLK, ROWS), 1)
    bias[...] = jnp.where(key <= row, 0.0, NEG).astype(F32)
    mx[...] = jnp.full(mx.shape, NEG, F32)
    lx[...] = jnp.zeros(lx.shape, F32)
    dx[...] = jnp.zeros(dx.shape, F32)
    for c, r in own_copies:
        r.wait()

    def stage_a(t, par, c):
        h, rows = t // 4, pl.ds(c * BLK, BLK)
        for u in range(2):
            ls = slice(u * ROWS, (u + 1) * ROWS)
            s = dot(kv[h, 0, rows, :], q_t[t * 2 + u])
            if c * BLK >= PROMPT:
                s = s + bias[...]
            s_buf[par][rows, ls] = s
            mx[par, :, ls] = jnp.maximum(mx[par, :, ls], fold(s, jnp.max))

    def stage_b(t, par, c):
        h, rows = t // 4, pl.ds(c * BLK, BLK)
        for u in range(2):
            ls = slice(u * ROWS, (u + 1) * ROWS)
            p = jnp.exp2(s_buf[par][rows, ls] * F32(SCALE * LOG2E) - ms[par, 0:1, ls])
            lx[par, :, ls] += fold(p, jnp.sum)
            p_buf[par][rows, ls] = p.astype(BF)
            d = dot(kv[h, 1, rows, :], g_t[t * 2 + u])
            d_buf[par][rows, ls] = d
            dx[par, :, ls] += fold(p * d, jnp.sum)

    def stage_c(t, par, c):
        h, rows = t // 4, pl.ds(c * BLK, BLK)
        p = p_buf[par][rows, :]
        ds = p * (d_buf[par][rows, :] - ds_[par, 0:1, :]).astype(BF)
        acc[1, :, rows] += dot(gs[par], p.T)
        acc[0, :, rows] += dot(qs[par], ds.T)
        dq_acc[...] += dot(k_t[h, :, rows], ds)

    def max_done(par):
        m = jnp.max(mx[par], axis=0, keepdims=True) * F32(SCALE * LOG2E)
        ms[par] = jnp.broadcast_to(m, (8, W))
        mx[par] = jnp.full((8, W), NEG, F32)

    def sums_done(t, par):
        r = 1.0 / jnp.sum(lx[par], axis=0, keepdims=True)
        ds_[par] = jnp.broadcast_to(jnp.sum(dx[par], axis=0, keepdims=True) * r, (8, W))
        rs[par] = jnp.broadcast_to(r, (8, W))
        lx[par] = jnp.zeros((8, W), F32)
        dx[par] = jnp.zeros((8, W), F32)
        for u in range(2):
            ls = slice(u * ROWS, (u + 1) * ROWS)
            gs[par, :, ls] = (g_t[t * 2 + u].astype(F32) * r[:, ls]).astype(BF)
            qs[par, :, ls] = (q_t[t * 2 + u].astype(F32) * r[:, ls]).astype(BF)

    def dq_copy(t, par):
        return pltpu.make_async_copy(dq_out.at[par], dq_hbm.at[:, lanes(2 * t, 2)], dq_sem.at[par])

    def dq_done(t, par):
        for u in range(2):
            ls = slice(u * ROWS, (u + 1) * ROWS)
            x = dq_acc[:, ls] * (rs[par, 0:1, ls] * F32(SCALE))
            dq_out[par, :, u * D : (u + 1) * D] = x.astype(BF).T
        dq_copy(t, par).start()

    def step(t, par, a=True, b=True, c=True, wait_dq=True):
        if c:
            dq_acc[...] = jnp.zeros((D, W), F32)
            sums_done(t - 2, par)
        if b:
            max_done(1 - par)
        for k in range(SPAN // BLK):
            if a:
                stage_a(t, par, k)
            if b:
                stage_b(t - 1, 1 - par, k)
            if c:
                stage_c(t - 2, par, k)
        if c:
            if wait_dq is True:
                dq_copy(t - 4, par).wait()
            elif wait_dq is not False:

                @pl.when(wait_dq)
                def _():
                    dq_copy(t - 4, par).wait()

            dq_done(t - 2, par)

    def resp_copy(h, w):
        out = (dkr_hbm, dvr_hbm)[w]
        return pltpu.make_async_copy(part.at[h, w, pl.ds(PROMPT, ROWS), :], out.at[:, lanes(h)], fin_sem.at[h, w])

    def sum_copy(h, w):
        out = (dkp_hbm, dvp_hbm)[w]
        return pltpu.make_async_copy(fin_out.at[h, w], out.at[:, lanes(h)], fin_sem.at[h, 2 + w])

    def swap(h):
        return remote(part.at[h, :, theirs, :], sib.at[h], sx_send.at[h], sx_recv.at[h], sibling)

    def scatter_1(h):
        part[h, 0] = (acc[0] * F32(SCALE)).astype(BF).T
        part[h, 1] = acc[1].astype(BF).T
        acc[...] = jnp.zeros(acc.shape, F32)
        swap(h).start()
        for w in range(2):
            resp_copy(h, w).start()

    def scatter_2(h):
        swap(h).wait_recv()
        for w in range(2):
            comb[h, w] = (part[h, w, mine, :].astype(F32) + sib[h, w].astype(F32)).astype(BF)
        for o in range(1, CHIPS):
            to = lax.rem(chip + o, CHIPS)
            rows = pl.ds(pl.multiple_of(to * SHARD, SHARD), SHARD)
            remote(comb.at[h, :, rows, :], land.at[h, CHIPS - 1 - o], sc_send.at[h], sc_recv.at[h], peer(o)).start()

    def scatter_3(h):
        x = land.at[h]
        pltpu.make_async_copy(x, x, sc_recv.at[h]).wait()
        rows = pl.ds(pl.multiple_of(chip * SHARD, SHARD), SHARD)
        for w in range(2):
            total = comb[h, w, rows, :].astype(F32)
            for o in range(CHIPS - 1):
                total = total + land[h, o, w].astype(F32)
            fin_out[h, w] = total.astype(BF)
            sum_copy(h, w).start()

    relay(0)
    keys_ready(0)
    step(0, 0, b=False, c=False)
    step(1, 1, c=False)

    def four(z, _):
        t = 4 * z + 2
        relay(z + 1)

        @pl.when(z > 0)
        def _():
            scatter_1(z - 1)

        @pl.when(z > 1)
        def _():
            scatter_3(z - 2)

        step(t, 0, wait_dq=z > 0)
        step(t + 1, 1, wait_dq=z > 0)
        keys_ready(z + 1)

        @pl.when(z > 0)
        def _():
            scatter_2(z - 1)

        step(t + 2, 0)
        step(t + 3, 1)
        return 0

    lax.fori_loop(0, HK - 1, four, 0)
    scatter_1(HK - 2)
    scatter_3(HK - 3)
    step(14, 0)
    step(15, 1)
    scatter_2(HK - 2)
    step(16, 0, a=False)
    step(17, 1, a=False, b=False)
    scatter_1(HK - 1)
    scatter_3(HK - 2)
    scatter_2(HK - 1)
    scatter_3(HK - 1)

    dq_copy(PAIRS - 2, 0).wait()
    dq_copy(PAIRS - 1, 1).wait()
    for h in range(HK):
        x = seven(h)
        pltpu.make_async_copy(x, x, ag_send.at[h]).wait()
        y = kv.at[h, :, mine, :]
        remote(y, y, rl_send.at[h], rl_recv.at[h], sibling).wait_send()
        swap(h).wait_send()
        x = land.at[h]
        pltpu.make_async_copy(x, x, sc_send.at[h]).wait()
        for w in range(2):
            resp_copy(h, w).wait()
            sum_copy(h, w).wait()


def shards(queries, keys_resp, values_resp, keys_prompt, values_prompt, grad_out, resp_len):
    vm = pltpu.VMEM
    dma = pltpu.SemaphoreType.DMA
    wide = HK * D
    hbm = pl.BlockSpec(memory_space=pl.ANY)
    return pl.pallas_call(
        kernel,
        out_shape=(
            jax.ShapeDtypeStruct((ROWS, HK * G * D), BF),
            jax.ShapeDtypeStruct((ROWS, wide), BF),
            jax.ShapeDtypeStruct((ROWS, wide), BF),
            jax.ShapeDtypeStruct((SHARD, wide), BF),
            jax.ShapeDtypeStruct((SHARD, wide), BF),
        ),
        in_specs=[hbm] * 6 + [pl.BlockSpec(memory_space=pltpu.SMEM)],
        out_specs=(hbm,) * 5,
        scratch_shapes=[
            vm((ROWS, HK * G * D), BF),
            vm((ROWS, HK * G * D), BF),
            vm((HK, 2, SPAN, D), BF),
            vm((SPAN, W), F32), vm((SPAN, W), F32),
            vm((SPAN, W), F32), vm((SPAN, W), F32),
            vm((SPAN, W), BF), vm((SPAN, W), BF),
            vm((2, 8, W), F32), vm((2, 8, W), F32), vm((2, 8, W), F32),
            vm((2, 8, W), F32), vm((2, 8, W), F32), vm((2, 8, W), F32),
            vm((HK * G, D, ROWS), BF), vm((HK * G, D, ROWS), BF),
            vm((HK, D, SPAN), BF),
            vm((2, D, W), BF), vm((2, D, W), BF),
            vm((D, W), F32),
            vm((BLK, ROWS), F32),
            vm((2, D, SPAN), F32),
            vm((2, ROWS, 2 * D), BF),
            vm((HK, 2, SPAN, D), BF),
            vm((HK, 2, HALF, D), BF),
            vm((HK, 2, HALF, D), BF),
            vm((HK, CHIPS - 1, 2, SHARD, D), BF),
            vm((HK, 2, SHARD, D), BF),
            dma((2,)), dma((HK, 2, 2)), dma((2,)), dma((HK, 4)),
            dma((HK,)), dma((HK,)), dma((HK,)), dma((HK,)), dma((HK,)), dma((HK,)), dma((HK,)), dma((HK,)),
        ],
        compiler_params=pltpu.CompilerParams(
            collective_id=0, has_side_effects=True, vmem_limit_bytes=56 * 2**20
        ),
    )(queries, grad_out, keys_resp, values_resp, keys_prompt, values_prompt, resp_len)


def solution(mesh):
    rows = P(("grp", "seq"), None)
    return jax.shard_map(
        shards,
        mesh=mesh,
        in_specs=(rows,) * 6 + (P(("grp", "seq")),),
        out_specs=(rows,) * 5,
        check_vma=False,
    )
```

time: 294 us -> 64.3 us (0.22); the launches traced: 290 us -> 64.1 us
  waiting for transfers between devices: 182 us -> 0 us
  Pallas kernels: 0 us -> 56.9 us
  matrix products: 37.9 us -> 0 us
  local copies, waits for them, and re-layouts: 32.5 us -> 5.87 us
  other arithmetic: 22.6 us -> 0 us
  between operations: 14.5 us -> 1.32 us
    reduce_scatter x2 -> x0, waiting for transfers between devices: 117 us -> none  [the longest x1 62.7 us: shards(): lax.psum_scatter(key_sums[:prompt_n].astype(jnp.bfloat16), 'seq', scatter...]
    all_gather x2 -> x0, waiting for transfers between devices: 63.7 us -> none  [the longest x1 31.9 us: shards(): lax.all_gather(keys_prompt, 'seq', axis=0, tiled=True)]
    pallas_call x0 -> x1, Pallas kernels: none -> 56.9 us  [shards(): pl.pallas_call(kernel, out_shape=(jax.ShapeDtypeStruct((ROWS, HK * G * D)...]
    dot_general x20 -> x0, matrix products: 37.9 us -> none  [the longest x4 11.8 us: per_head(): jnp.einsum('rgd,ld->grl', grad_head, value_head, preferred_element_type=j...]
    dynamic_slice x12 -> x0, local copies, waits for them, and re-layouts: 9.48 us -> none  [the longest x8 5.15 us: per_head(): lax.dynamic_slice_in_dim(query_rows, head_idx * group_width, group_width, 1)]
    convert_element_type x4 -> x0, other arithmetic: 8.24 us -> none  [per_head(): scores_low = grad_scores.astype(jnp.bfloat16)]
    while x16 -> x0, local copies, waits for them, and re-layouts: 5.86 us -> none
    slice x4 -> x0, local copies, waits for them, and re-layouts: 5.85 us -> none  [the longest x1 2.37 us: shards(): value_sums[:prompt_n].astype(jnp.bfloat16)]
  transfers between devices with their start and end apart: 4 -> 0, of which waited for: 4 -> 0; matrix products, arithmetic and copies ran while one was open for 4% -> 0% of each run, Pallas kernels for 0% -> 0%
where the time goes in v1:
time: 64.3 us; the launch traced here: 64.1 us
  Pallas kernels  56.9 us (88%)
  local copies, waits for them, and re-layouts  5.87 us (9%)
  between operations  1.32 us (2%)
    pallas_call x1, Pallas kernels, shards(): pl.pallas_call(kernel, out_shape=(jax.ShapeDtypeStruct((ROWS, HK * G * D)...  56.9 us
    unnamed x13, local copies, waits for them, and re-layouts  5.87 us

profile of v1, /device:TPU:1, one launch (start us, length us, event | category | flops | bytes accessed | tf_op | source)
XLA Modules:
  0.0 64.1 jit_solution(13968711121266368784)
XLA Ops:
  1.3 56.9 %shard_map.110 = (bf16[256,4096]{1,0:T(8,128)(2,1)}, bf16[256,512]{1,0:T(8,128)(2,1)}, bf16[256,512]{1,0:T(8,128)(2,1)}, bf16[64,512]{1,0:T(8,128)(2,1)}, bf16[64,512]{1,0:T(8,128)(2,1)}) custom-call(bf16[256,4096]{1,0:T(8,128)(2,1)} %q_hbm.1, bf16[256,4096]{1,0:T(8,128)(2,1)} %g_hbm.1, bf16[256,512]{1,0:T(8,128)(2,1)} %kr_hbm.1, bf16[256,512]{1,0:T(8,128)(2,1)} %vr_hbm.1, ...), custom_call_target="tpu_custom_call" | custom-call | tf_op jit(solution)/shard_map/pallas_call | solution.py:311
  58.2 0.0 copy-start.1
  58.2 0.0 copy-start
  58.2 0.0 copy-start.3
  58.2 0.0 copy-start.2
  58.2 3.2 %copy.18 = bf16[256,4096]{1,0:T(8,128)(2,1)} copy(bf16[256,4096]{1,0:T(8,128)(2,1)} %get-tuple-element.10) | data formatting | bytes 4194304
  61.4 0.0 copy-done.1
  61.4 0.7 %copy.19 = bf16[256,512]{1,0:T(8,128)(2,1)} copy(bf16[256,512]{1,0:T(8,128)(2,1)S(1)} %copy-done.1) | data formatting | bytes 524288
  62.1 0.0 copy-done
  62.1 0.7 %copy.20 = bf16[256,512]{1,0:T(8,128)(2,1)} copy(bf16[256,512]{1,0:T(8,128)(2,1)S(1)} %copy-done) | data formatting | bytes 524288
  62.8 0.0 copy-done.3
  62.9 0.6 copy.21
  63.5 0.0 copy-done.2
  63.5 0.6 copy.22
Async XLA Ops:
  58.2 3.2 %copy-start.1 = (bf16[256,512]{1,0:T(8,128)(2,1)S(1)}, bf16[256,512]{1,0:T(8,128)(2,1)}, u32[]{:S(2)}) copy-start(bf16[256,512]{1,0:T(8,128)(2,1)} %get-tuple-element.11) | copy-start | bytes 786436
  58.2 3.9 %copy-start = (bf16[256,512]{1,0:T(8,128)(2,1)S(1)}, bf16[256,512]{1,0:T(8,128)(2,1)}, u32[]{:S(2)}) copy-start(bf16[256,512]{1,0:T(8,128)(2,1)} %get-tuple-element.12) | copy-start | bytes 786436
  58.2 4.6 %copy-start.3 = (bf16[64,512]{1,0:T(8,128)(2,1)S(1)}, bf16[64,512]{1,0:T(8,128)(2,1)}, u32[]{:S(2)}) copy-start(bf16[64,512]{1,0:T(8,128)(2,1)} %get-tuple-element.13) | copy-start | bytes 196612
  58.2 5.2 %copy-start.2 = (bf16[64,512]{1,0:T(8,128)(2,1)S(1)}, bf16[64,512]{1,0:T(8,128)(2,1)}, u32[]{:S(2)}) copy-start(bf16[64,512]{1,0:T(8,128)(2,1)} %get-tuple-element.14) | copy-start | bytes 196612

commit v2 on v1

v2 whole, which is shorter than its diff:
```python
import functools

import jax
import jax.numpy as jnp
from jax import lax
from jax.experimental import pallas as pl
from jax.experimental.pallas import tpu as pltpu
from jax.sharding import PartitionSpec as P

D = 128
HK = 4
G = 8
ROWS = 256
PROMPT = 1024
SPAN = PROMPT + ROWS
SHARD = 64
CHIPS = 8
HALF = CHIPS * SHARD
PAIRS = HK * G // 2
BLK = 256
W = 2 * ROWS
SCALE = D**-0.5
LOG2E = 1.4426950408889634
NEG = -1e30
BF = jnp.bfloat16
F32 = jnp.float32


def dot(a, b):
    return lax.dot_general(a, b, (((1,), (0,)), ((), ())), preferred_element_type=F32)


def fold(x, op):
    return op(x.reshape(x.shape[0] // 8, 8, x.shape[1]), axis=0)


def lanes(i, n=1):
    return pl.ds(pl.multiple_of(i * D, D), n * D)


def kernel(
    q_hbm, g_hbm, kr_hbm, vr_hbm, kp_hbm, vp_hbm, len_ref,
    dq_ref, dkr_ref, dvr_ref, dkp_ref, dvp_ref,
    kv, s0, s1, d0, d1, p0, p1, dsb, mx, lx, dx, ms, ds_, rs, q_t, g_t, k_t, gs, qs,
    bias, acc, part, sib, comb, land,
    in_sem, own_sem, ag_send, ag_recv, rl_send, rl_recv, sx_send, sx_recv, sc_send, sc_recv,
):
    s_buf, d_buf, p_buf = [s0, s1], [d0, d1], [p0, p1]
    me = lax.axis_index("seq")
    core, chip = lax.rem(me, 2), me // 2
    sibling = me + 1 - 2 * core

    def peer(o):
        return 2 * lax.rem(chip + o, CHIPS) + core

    def remote(src, dst, send, recv, to):
        return pltpu.make_async_remote_copy(
            src_ref=src, dst_ref=dst, send_sem=send, recv_sem=recv,
            device_id={"seq": to}, device_id_type=pl.DeviceIdType.MESH,
        )

    own = pl.ds(pl.multiple_of(core * HALF + chip * SHARD, SHARD), SHARD)
    mine = pl.ds(pl.multiple_of(core * HALF, HALF), HALF)
    theirs = pl.ds(pl.multiple_of((1 - core) * HALF, HALF), HALF)

    own_copies = []
    for h in range(HK):
        for w, (p_hbm, r_hbm) in enumerate(((kp_hbm, kr_hbm), (vp_hbm, vr_hbm))):
            col = pl.ds(h * D, D)
            c = pltpu.make_async_copy(p_hbm.at[:, col], kv.at[h, w, own, :], own_sem.at[h, w, 0])
            c.start()
            r = pltpu.make_async_copy(r_hbm.at[:, col], kv.at[h, w, pl.ds(PROMPT, ROWS), :], own_sem.at[h, w, 1])
            r.start()
            own_copies.append((c, r))
    q_copy = pltpu.make_async_copy(q_hbm, dq_ref, in_sem.at[0])
    q_copy.start()
    g_copies = []
    for j in range(HK * G * D // W):
        to = dsb.at[PAIRS - 2 + j // 4, pl.ds(j % 4 * ROWS, ROWS), :]
        g_copies.append(pltpu.make_async_copy(g_hbm.at[:, pl.ds(j * W, W)], to, in_sem.at[1 + j]))
        g_copies[-1].start()

    barrier = pltpu.get_barrier_semaphore()
    for o in range(1, CHIPS):
        pl.semaphore_signal(barrier, inc=1, device_id={"seq": peer(o)}, device_id_type=pl.DeviceIdType.MESH)
    pl.semaphore_signal(barrier, inc=1, device_id={"seq": sibling}, device_id_type=pl.DeviceIdType.MESH)
    pl.semaphore_wait(barrier, CHIPS)

    def sends(h, w):
        blk = kv.at[h, w, own, :]
        for o in range(1, CHIPS):
            remote(blk, blk, ag_send.at[h, w], ag_recv.at[h, w], peer(o)).start()

    def seven(h, w):
        return kv.at[h, w, pl.ds(0, (CHIPS - 1) * SHARD), :]

    def relay(h, w):
        x = seven(h, w)
        pltpu.make_async_copy(x, x, ag_recv.at[h, w]).wait()
        y = kv.at[h, w, mine, :]
        remote(y, y, rl_send.at[h, w], rl_recv.at[h, w], sibling).start()

    def relayed(h, w):
        y = kv.at[h, w, theirs, :]
        remote(y, y, rl_send.at[h, w], rl_recv.at[h, w], sibling).wait_recv()

    own_copies[0][0].wait()
    sends(0, 0)
    own_copies[1][0].wait()
    sends(0, 1)
    for c, _ in own_copies[2:]:
        c.wait()

    q_copy.wait()
    for c in g_copies:
        c.wait()
    live = lax.broadcasted_iota(jnp.int32, (D, ROWS), 1) < len_ref[0]

    def prep(i, _):
        q_t[i] = dq_ref[:, lanes(i)].T
        from_row = pl.ds(pl.multiple_of(i // 4 % 4 * ROWS, ROWS), ROWS)
        gt = dsb[PAIRS - 2 + i // 16, from_row, lanes(i % 4)].T.astype(F32)
        g_t[i] = jnp.where(live, gt, 0.0).astype(BF)
        return 0

    def prep_four(i, _):
        for u in range(4):
            prep(4 * i + u, 0)
        return 0

    prep(0, 0)
    prep(1, 0)
    acc[...] = jnp.zeros(acc.shape, F32)
    key = lax.broadcasted_iota(jnp.int32, (BLK, ROWS), 0)
    row = lax.broadcasted_iota(jnp.int32, (BLK, ROWS), 1)
    bias[...] = jnp.where(key <= row, 0.0, NEG).astype(F32)
    mx[...] = jnp.full(mx.shape, NEG, F32)
    lx[...] = jnp.zeros(lx.shape, F32)
    dx[...] = jnp.zeros(dx.shape, F32)
    for c, r in own_copies:
        r.wait()

    def stage_a(t, par, c):
        h, rows = t // 4, pl.ds(c * BLK, BLK)
        for u in range(2):
            ls = slice(u * ROWS, (u + 1) * ROWS)
            s = dot(kv[h, 0, rows, :], q_t[t * 2 + u])
            if c * BLK >= PROMPT:
                s = s + bias[...]
            s_buf[par][rows, ls] = s
            mx[par, :, ls] = jnp.maximum(mx[par, :, ls], fold(s, jnp.max))

    def stage_b(t, par, c):
        h, rows = t // 4, pl.ds(c * BLK, BLK)
        for u in range(2):
            ls = slice(u * ROWS, (u + 1) * ROWS)
            p = jnp.exp2(s_buf[par][rows, ls] * F32(SCALE * LOG2E) - ms[par, 0:1, ls])
            lx[par, :, ls] += fold(p, jnp.sum)
            p_buf[par][rows, ls] = p.astype(BF)
            d = dot(kv[h, 1, rows, :], g_t[t * 2 + u])
            d_buf[par][rows, ls] = d
            dx[par, :, ls] += fold(p * d, jnp.sum)

    def stage_c(t, par, c):
        rows = pl.ds(c * BLK, BLK)
        p = p_buf[par][rows, :]
        ds = p * (d_buf[par][rows, :] - ds_[par, 0:1, :]).astype(BF)
        dsb[t, rows, :] = ds
        acc[1, :, rows] += dot(gs[par], p.T)
        acc[0, :, rows] += dot(qs[par], ds.T)

    def max_done(par):
        m = jnp.max(mx[par], axis=0, keepdims=True) * F32(SCALE * LOG2E)
        ms[par] = jnp.broadcast_to(m, (8, W))
        mx[par] = jnp.full((8, W), NEG, F32)

    def sums_done(t, par):
        r = 1.0 / jnp.sum(lx[par], axis=0, keepdims=True)
        ds_[par] = jnp.broadcast_to(jnp.sum(dx[par], axis=0, keepdims=True) * r, (8, W))
        rs[t] = jnp.broadcast_to(r * F32(SCALE), (8, W))
        lx[par] = jnp.zeros((8, W), F32)
        dx[par] = jnp.zeros((8, W), F32)
        for u in range(2):
            ls = slice(u * ROWS, (u + 1) * ROWS)
            gs[par, :, ls] = (g_t[t * 2 + u].astype(F32) * r[:, ls]).astype(BF)
            qs[par, :, ls] = (q_t[t * 2 + u].astype(F32) * r[:, ls]).astype(BF)

    def grad_queries(h):
        k_t[...] = kv[h, 0].T
        for j in range(PAIRS // HK):
            t = h * (PAIRS // HK) + j
            x = dot(k_t[...], dsb[t]) * rs[t, 0:1, :]
            for u in range(2):
                dq_ref[:, lanes(2 * t + u)] = x[:, u * ROWS : (u + 1) * ROWS].astype(BF).T

    def step(t, par, a=True, b=True, c=True):
        if c:
            sums_done(t - 2, par)
        if b:
            max_done(1 - par)
        for k in range(SPAN // BLK):
            if a:
                stage_a(t, par, k)
            if b:
                stage_b(t - 1, 1 - par, k)
            if c:
                stage_c(t - 2, par, k)

    def swap(h):
        return remote(part.at[h, :, theirs, :], sib.at[h], sx_send.at[h], sx_recv.at[h], sibling)

    def scatter_1(h):
        part[h, 0] = (acc[0] * F32(SCALE)).astype(BF).T
        part[h, 1] = acc[1].astype(BF).T
        acc[...] = jnp.zeros(acc.shape, F32)
        swap(h).start()
        dkr_ref[:, lanes(h)] = part[h, 0, PROMPT:, :]
        dvr_ref[:, lanes(h)] = part[h, 1, PROMPT:, :]

    def scatter_2(h):
        swap(h).wait_recv()
        for w in range(2):
            comb[h, w] = (part[h, w, mine, :].astype(F32) + sib[h, w].astype(F32)).astype(BF)
        for o in range(1, CHIPS):
            to = lax.rem(chip + o, CHIPS)
            rows = pl.ds(pl.multiple_of(to * SHARD, SHARD), SHARD)
            remote(comb.at[h, :, rows, :], land.at[h, CHIPS - 1 - o], sc_send.at[h], sc_recv.at[h], peer(o)).start()

    def scatter_3(h):
        x = land.at[h]
        pltpu.make_async_copy(x, x, sc_recv.at[h]).wait()
        rows = pl.ds(pl.multiple_of(chip * SHARD, SHARD), SHARD)
        for w, out in enumerate((dkp_ref, dvp_ref)):
            total = comb[h, w, rows, :].astype(F32)
            for o in range(CHIPS - 1):
                total = total + land[h, o, w].astype(F32)
            out[:, lanes(h)] = total.astype(BF)

    relay(0, 0)
    sends(1, 0)
    sends(1, 1)
    lax.fori_loop(0, HK * G // 4, prep_four, 0)
    relayed(0, 0)
    step(0, 0, b=False, c=False)
    relay(0, 1)
    relayed(0, 1)
    step(1, 1, c=False)

    def four(z, _):
        t = 4 * z + 2
        relay(z + 1, 0)
        relay(z + 1, 1)

        @pl.when(z < HK - 2)
        def _():
            sends(z + 2, 0)
            sends(z + 2, 1)

        @pl.when(z > 0)
        def _():
            scatter_1(z - 1)

        step(t, 0)
        step(t + 1, 1)
        relayed(z + 1, 0)
        relayed(z + 1, 1)

        @pl.when(z > 0)
        def _():
            scatter_2(z - 1)

        @pl.when(z > 1)
        def _():
            scatter_3(z - 2)

        step(t + 2, 0)
        step(t + 3, 1)
        return 0

    lax.fori_loop(0, HK - 1, four, 0)
    scatter_1(HK - 2)
    step(14, 0)
    step(15, 1)
    scatter_2(HK - 2)
    scatter_3(HK - 3)
    step(16, 0, a=False)
    step(17, 1, a=False, b=False)
    scatter_1(HK - 1)
    grad_queries(0)
    scatter_2(HK - 1)
    grad_queries(1)
    scatter_3(HK - 2)
    grad_queries(2)
    grad_queries(3)
    scatter_3(HK - 1)

    for h in range(HK):
        for w in range(2):
            x = seven(h, w)
            pltpu.make_async_copy(x, x, ag_send.at[h, w]).wait()
            y = kv.at[h, w, mine, :]
            remote(y, y, rl_send.at[h, w], rl_recv.at[h, w], sibling).wait_send()
        swap(h).wait_send()
        x = land.at[h]
        pltpu.make_async_copy(x, x, sc_send.at[h]).wait()


def publish(*refs):
    n = len(refs) // 2
    copies = [pltpu.make_async_copy(refs[i], refs[n + i], refs[-1].at[i]) for i in range(n)]
    for c in copies:
        c.start()
    for c in copies:
        c.wait()


def shards(queries, keys_resp, values_resp, keys_prompt, values_prompt, grad_out, resp_len):
    vm = pltpu.VMEM
    dma = pltpu.SemaphoreType.DMA
    wide = HK * D
    hbm = pl.BlockSpec(memory_space=pl.ANY)
    outs = pl.pallas_call(
        kernel,
        out_shape=(
            vm((ROWS, HK * G * D), BF),
            vm((ROWS, wide), BF),
            vm((ROWS, wide), BF),
            vm((SHARD, wide), BF),
            vm((SHARD, wide), BF),
        ),
        in_specs=[hbm] * 6 + [pl.BlockSpec(memory_space=pltpu.SMEM)],
        out_specs=(pl.BlockSpec(memory_space=vm),) * 5,
        scratch_shapes=[
            vm((HK, 2, SPAN, D), BF),
            vm((SPAN, W), F32), vm((SPAN, W), F32),
            vm((SPAN, W), F32), vm((SPAN, W), F32),
            vm((SPAN, W), BF), vm((SPAN, W), BF),
            vm((PAIRS, SPAN, W), BF),
            vm((2, 8, W), F32), vm((2, 8, W), F32), vm((2, 8, W), F32),
            vm((2, 8, W), F32), vm((2, 8, W), F32), vm((PAIRS, 8, W), F32),
            vm((HK * G, D, ROWS), BF), vm((HK * G, D, ROWS), BF),
            vm((D, SPAN), BF),
            vm((2, D, W), BF), vm((2, D, W), BF),
            vm((BLK, ROWS), F32),
            vm((2, D, SPAN), F32),
            vm((HK, 2, SPAN, D), BF),
            vm((HK, 2, HALF, D), BF),
            vm((HK, 2, HALF, D), BF),
            vm((HK, CHIPS - 1, 2, SHARD, D), BF),
            dma((9,)), dma((HK, 2, 2)),
            dma((HK, 2)), dma((HK, 2)), dma((HK, 2)), dma((HK, 2)), dma((HK,)), dma((HK,)), dma((HK,)), dma((HK,)),
        ],
        compiler_params=pltpu.CompilerParams(
            collective_id=0, has_side_effects=True, vmem_limit_bytes=56 * 2**20
        ),
    )(queries, grad_out, keys_resp, values_resp, keys_prompt, values_prompt, resp_len)
    return pl.pallas_call(
        publish,
        out_shape=tuple(jax.ShapeDtypeStruct(o.shape, o.dtype) for o in outs),
        in_specs=[pl.BlockSpec(memory_space=vm)] * 5,
        out_specs=(hbm,) * 5,
        scratch_shapes=[dma((5,))],
    )(*[pltpu.with_memory_space_constraint(o, vm) for o in outs])


def solution(mesh):
    rows = P(("grp", "seq"), None)
    return jax.shard_map(
        shards,
        mesh=mesh,
        in_specs=(rows,) * 6 + (P(("grp", "seq")),),
        out_specs=(rows,) * 5,
        check_vma=False,
    )
```

time: 64.3 us -> 52.8 us (0.82)
  local copies, waits for them, and re-layouts: 5.87 us -> 0 us
  Pallas kernels: 56.9 us -> 51.2 us
    unnamed x13 -> x0, local copies, waits for them, and re-layouts: 5.87 us -> none
    pallas_call x1 -> x2, Pallas kernels: 56.9 us -> 51.2 us  [the longest x1 49.6 us: shards(): pl.pallas_call(kernel, out_shape=(vm((ROWS, HK * G * D), BF), vm((ROWS, w...]
where the time goes in v2:
time: 52.8 us; the launch traced here: 52.6 us
  Pallas kernels  51.2 us (97%)
  between operations  1.45 us (3%)
    pallas_call x1, Pallas kernels, shards(): pl.pallas_call(kernel, out_shape=(vm((ROWS, HK * G * D), BF), vm((ROWS, w...  49.6 us
    pallas_call x1, Pallas kernels, shards(): pl.pallas_call(publish, out_shape=tuple((jax.ShapeDtypeStruct(o.shape, o....  1.56 us

profile of v2, /device:TPU:1, one launch (start us, length us, event | category | flops | bytes accessed | tf_op | source)
XLA Modules:
  0.0 52.6 jit_solution(2923257070364528956)
XLA Ops:
  1.3 49.6 %shard_map.110 = (bf16[256,4096]{1,0:T(8,128)(2,1)S(1)}, bf16[256,512]{1,0:T(8,128)(2,1)S(1)}, bf16[256,512]{1,0:T(8,128)(2,1)S(1)}, bf16[64,512]{1,0:T(8,128)(2,1)S(1)}, bf16[64,512]{1,0:T(8,128)(2,1)S(1)}) custom-call(bf16[256,4096]{1,0:T(8,128)(2,1)} %q_hbm.1, bf16[256,4096]{1,0:T(8,128)(2,1)} %g_hbm.1, bf16[256,512]{1,0:T(8,128)(2,1)} %kr_hbm.1, ...), custom_call_target="tpu_custom_call" | custom-call | tf_op jit(solution)/shard_map/pallas_call | solution.py:322
  50.9 1.6 %shard_map.111 = (bf16[256,4096]{1,0:T(8,128)(2,1)}, bf16[256,512]{1,0:T(8,128)(2,1)}, bf16[256,512]{1,0:T(8,128)(2,1)}, bf16[64,512]{1,0:T(8,128)(2,1)}, bf16[64,512]{1,0:T(8,128)(2,1)}) custom-call(bf16[256,4096]{1,0:T(8,128)(2,1)S(1)} %get-tuple-element.10.refs_0_, bf16[256,512]{1,0:T(8,128)(2,1)S(1)} %get-tuple-element.11.refs_1_, ...), custom_call_target="tpu_custom_call" | custom-call | tf_op jit(solution)/shard_map/pallas_call | solution.py:357

commit v3 on v2

--- a/solution.py
+++ b/solution.py
@@ -18,6 +18,7 @@
 HALF = CHIPS * SHARD
 PAIRS = HK * G // 2
 BLK = 256
+SUB = 64
 W = 2 * ROWS
 SCALE = D**-0.5
 LOG2E = 1.4426950408889634
@@ -42,7 +43,7 @@
     q_hbm, g_hbm, kr_hbm, vr_hbm, kp_hbm, vp_hbm, len_ref,
     dq_ref, dkr_ref, dvr_ref, dkp_ref, dvp_ref,
     kv, s0, s1, d0, d1, p0, p1, dsb, mx, lx, dx, ms, ds_, rs, q_t, g_t, k_t, gs, qs,
-    bias, acc, part, sib, comb, land,
+    p_t, bias, acc, part, sib, land,
     in_sem, own_sem, ag_send, ag_recv, rl_send, rl_recv, sx_send, sx_recv, sc_send, sc_recv,
 ):
     s_buf, d_buf, p_buf = [s0, s1], [d0, d1], [p0, p1]
@@ -117,7 +118,10 @@
     live = lax.broadcasted_iota(jnp.int32, (D, ROWS), 1) < len_ref[0]
 
     def prep(i, _):
-        q_t[i] = dq_ref[:, lanes(i)].T
+        qt = dq_ref[:, lanes(i)].T.astype(F32) * F32(SCALE * LOG2E)
+        high = qt.astype(BF)
+        q_t[i, 0:D, :] = high
+        q_t[i, D : 2 * D, :] = (qt - high.astype(F32)).astype(BF)
         from_row = pl.ds(pl.multiple_of(i // 4 % 4 * ROWS, ROWS), ROWS)
         gt = dsb[PAIRS - 2 + i // 16, from_row, lanes(i % 4)].T.astype(F32)
         g_t[i] = jnp.where(live, gt, 0.0).astype(BF)
@@ -128,8 +132,6 @@
             prep(4 * i + u, 0)
         return 0
 
-    prep(0, 0)
-    prep(1, 0)
     acc[...] = jnp.zeros(acc.shape, F32)
     key = lax.broadcasted_iota(jnp.int32, (BLK, ROWS), 0)
     row = lax.broadcasted_iota(jnp.int32, (BLK, ROWS), 1)
@@ -144,7 +146,8 @@
         h, rows = t // 4, pl.ds(c * BLK, BLK)
         for u in range(2):
             ls = slice(u * ROWS, (u + 1) * ROWS)
-            s = dot(kv[h, 0, rows, :], q_t[t * 2 + u])
+            k = kv[h, 0, rows, :]
+            s = dot(jnp.concatenate([k, k], axis=1), q_t[t * 2 + u])
             if c * BLK >= PROMPT:
                 s = s + bias[...]
             s_buf[par][rows, ls] = s
@@ -154,23 +157,40 @@
         h, rows = t // 4, pl.ds(c * BLK, BLK)
         for u in range(2):
             ls = slice(u * ROWS, (u + 1) * ROWS)
-            p = jnp.exp2(s_buf[par][rows, ls] * F32(SCALE * LOG2E) - ms[par, 0:1, ls])
-            lx[par, :, ls] += fold(p, jnp.sum)
-            p_buf[par][rows, ls] = p.astype(BF)
             d = dot(kv[h, 1, rows, :], g_t[t * 2 + u])
-            d_buf[par][rows, ls] = d
-            dx[par, :, ls] += fold(p * d, jnp.sum)
+            top, l_sum, d_sum = ms[par, 0:1, ls], lx[par, :, ls], dx[par, :, ls]
+            for i in range(0, BLK, SUB):
+                sub = pl.ds(c * BLK + i, SUB)
+                p = jnp.exp2(s_buf[par][sub, ls] - top)
+                l_sum += fold(p, jnp.sum)
+                p_buf[par][sub, ls] = p.astype(BF)
+                d_buf[par][sub, ls] = d[i : i + SUB]
+                d_sum += fold(p * d[i : i + SUB], jnp.sum)
+            lx[par, :, ls] = l_sum
+            dx[par, :, ls] = d_sum
+
+    def value_terms(par, c):
+        rows = pl.ds(c * BLK, BLK)
+        p_t[c % 2] = p_buf[par][rows, :].T
+        acc[1, :, rows] += dot(gs[par], p_t[c % 2])
+
+    def key_terms(t, par, c):
+        rows = pl.ds(c * BLK, BLK)
+        for i in range(0, BLK, SUB):
+            sub = pl.ds(c * BLK + i, SUB)
+            for u in range(2):
+                ls = slice(u * ROWS, (u + 1) * ROWS)
+                ds = (d_buf[par][sub, ls] - ds_[par, 0:1, ls]).astype(BF)
+                dsb[t, sub, ls] = p_buf[par][sub, ls] * ds
+        return rows
 
     def stage_c(t, par, c):
-        rows = pl.ds(c * BLK, BLK)
-        p = p_buf[par][rows, :]
-        ds = p * (d_buf[par][rows, :] - ds_[par, 0:1, :]).astype(BF)
-        dsb[t, rows, :] = ds
-        acc[1, :, rows] += dot(gs[par], p.T)
-        acc[0, :, rows] += dot(qs[par], ds.T)
+        rows = key_terms(t, par, c)
+        value_terms(par, c)
+        acc[0, :, rows] += dot(qs[par], dsb[t, rows, :].T)
 
     def max_done(par):
-        m = jnp.max(mx[par], axis=0, keepdims=True) * F32(SCALE * LOG2E)
+        m = jnp.max(mx[par], axis=0, keepdims=True)
         ms[par] = jnp.broadcast_to(m, (8, W))
         mx[par] = jnp.full((8, W), NEG, F32)
 
@@ -183,7 +203,8 @@
         for u in range(2):
             ls = slice(u * ROWS, (u + 1) * ROWS)
             gs[par, :, ls] = (g_t[t * 2 + u].astype(F32) * r[:, ls]).astype(BF)
-            qs[par, :, ls] = (q_t[t * 2 + u].astype(F32) * r[:, ls]).astype(BF)
+            q = q_t[t * 2 + u, 0:D, :].astype(F32) + q_t[t * 2 + u, D : 2 * D, :].astype(F32)
+            qs[par, :, ls] = (q * r[:, ls]).astype(BF)
 
     def grad_queries(h):
         k_t[...] = kv[h, 0].T
@@ -206,93 +227,107 @@
             if c:
                 stage_c(t - 2, par, k)
 
-    def swap(h):
-        return remote(part.at[h, :, theirs, :], sib.at[h], sx_send.at[h], sx_recv.at[h], sibling)
-
-    def scatter_1(h):
-        part[h, 0] = (acc[0] * F32(SCALE)).astype(BF).T
-        part[h, 1] = acc[1].astype(BF).T
-        acc[...] = jnp.zeros(acc.shape, F32)
-        swap(h).start()
-        dkr_ref[:, lanes(h)] = part[h, 0, PROMPT:, :]
-        dvr_ref[:, lanes(h)] = part[h, 1, PROMPT:, :]
-
-    def scatter_2(h):
-        swap(h).wait_recv()
-        for w in range(2):
-            comb[h, w] = (part[h, w, mine, :].astype(F32) + sib[h, w].astype(F32)).astype(BF)
+    def swap(h, w):
+        return remote(part.at[h, w, theirs, :], sib.at[h, w], sx_send.at[h, w], sx_recv.at[h, w], sibling)
+
+    def scatter_1(h, w):
+        x = acc[w] * F32(1 / LOG2E) if w == 0 else acc[w]
+        part[h, w] = x.astype(BF).T
+        acc[w] = jnp.zeros(acc.shape[1:], F32)
+        swap(h, w).start()
+        out = (dkr_ref, dvr_ref)[w]
+        out[:, lanes(h)] = part[h, w, PROMPT:, :]
+
+    def scatter_2(h, w):
+        swap(h, w).wait_recv()
+        part[h, w, mine, :] = (part[h, w, mine, :].astype(F32) + sib[h, w].astype(F32)).astype(BF)
         for o in range(1, CHIPS):
             to = lax.rem(chip + o, CHIPS)
-            rows = pl.ds(pl.multiple_of(to * SHARD, SHARD), SHARD)
-            remote(comb.at[h, :, rows, :], land.at[h, CHIPS - 1 - o], sc_send.at[h], sc_recv.at[h], peer(o)).start()
-
-    def scatter_3(h):
-        x = land.at[h]
-        pltpu.make_async_copy(x, x, sc_recv.at[h]).wait()
-        rows = pl.ds(pl.multiple_of(chip * SHARD, SHARD), SHARD)
-        for w, out in enumerate((dkp_ref, dvp_ref)):
-            total = comb[h, w, rows, :].astype(F32)
-            for o in range(CHIPS - 1):
-                total = total + land[h, o, w].astype(F32)
-            out[:, lanes(h)] = total.astype(BF)
-
+            rows = pl.ds(pl.multiple_of(core * HALF + to * SHARD, SHARD), SHARD)
+            remote(
+                part.at[h, w, rows, :], land.at[h, w, CHIPS - 1 - o], sc_send.at[h, w], sc_recv.at[h, w], peer(o)
+            ).start()
+
+    def scatter_3(h, w):
+        x = land.at[h, w]
+        pltpu.make_async_copy(x, x, sc_recv.at[h, w]).wait()
+        total = part[h, w, own, :].astype(F32)
+        for o in range(CHIPS - 1):
+            total = total + land[h, w, o].astype(F32)
+        out = (dkp_ref, dvp_ref)[w]
+        out[:, lanes(h)] = total.astype(BF)
+
+    def both(f, h):
+        f(h, 1)
+        f(h, 0)
+
+    half = HK * G // 8
+    lax.fori_loop(0, half, prep_four, 0)
     relay(0, 0)
     sends(1, 0)
     sends(1, 1)
-    lax.fori_loop(0, HK * G // 4, prep_four, 0)
+    lax.fori_loop(half, 2 * half, prep_four, 0)
+    relay(0, 1)
     relayed(0, 0)
     step(0, 0, b=False, c=False)
-    relay(0, 1)
+    sends(2, 0)
+    sends(2, 1)
     relayed(0, 1)
     step(1, 1, c=False)
+    sends(3, 0)
+    sends(3, 1)
 
     def four(z, _):
         t = 4 * z + 2
+
+        @pl.when(z > 0)
+        def _():
+            both(scatter_1, z - 1)
+
+        step(t, 0)
         relay(z + 1, 0)
         relay(z + 1, 1)
-
-        @pl.when(z < HK - 2)
-        def _():
-            sends(z + 2, 0)
-            sends(z + 2, 1)
-
-        @pl.when(z > 0)
-        def _():
-            scatter_1(z - 1)
-
-        step(t, 0)
         step(t + 1, 1)
         relayed(z + 1, 0)
         relayed(z + 1, 1)
 
         @pl.when(z > 0)
         def _():
-            scatter_2(z - 1)
+            both(scatter_2, z - 1)
 
         @pl.when(z > 1)
         def _():
-            scatter_3(z - 2)
+            both(scatter_3, z - 2)
 
         step(t + 2, 0)
         step(t + 3, 1)
         return 0
 
     lax.fori_loop(0, HK - 1, four, 0)
-    scatter_1(HK - 2)
+    last = HK - 1
+    both(scatter_1, last - 1)
     step(14, 0)
     step(15, 1)
-    scatter_2(HK - 2)
-    scatter_3(HK - 3)
+    both(scatter_2, last - 1)
+    both(scatter_3, last - 2)
     step(16, 0, a=False)
-    step(17, 1, a=False, b=False)
-    scatter_1(HK - 1)
+    t, par = PAIRS - 1, 1
+    sums_done(t, par)
+    for k in range(SPAN // BLK):
+        value_terms(par, k)
+    scatter_1(last, 1)
+    for k in range(SPAN // BLK):
+        rows = key_terms(t, par, k)
+        acc[0, :, rows] += dot(qs[par], dsb[t, rows, :].T)
+    scatter_1(last, 0)
+    scatter_2(last, 1)
     grad_queries(0)
-    scatter_2(HK - 1)
+    scatter_2(last, 0)
     grad_queries(1)
-    scatter_3(HK - 2)
+    both(scatter_3, last - 1)
     grad_queries(2)
     grad_queries(3)
-    scatter_3(HK - 1)
+    both(scatter_3, last)
 
     for h in range(HK):
         for w in range(2):
@@ -300,9 +335,9 @@
             pltpu.make_async_copy(x, x, ag_send.at[h, w]).wait()
             y = kv.at[h, w, mine, :]
             remote(y, y, rl_send.at[h, w], rl_recv.at[h, w], sibling).wait_send()
-        swap(h).wait_send()
-        x = land.at[h]
-        pltpu.make_async_copy(x, x, sc_send.at[h]).wait()
+            swap(h, w).wait_send()
+            x = land.at[h, w]
+            pltpu.make_async_copy(x, x, sc_send.at[h, w]).wait()
 
 
 def publish(*refs):
@@ -338,17 +373,18 @@
             vm((PAIRS, SPAN, W), BF),
             vm((2, 8, W), F32), vm((2, 8, W), F32), vm((2, 8, W), F32),
             vm((2, 8, W), F32), vm((2, 8, W), F32), vm((PAIRS, 8, W), F32),
-            vm((HK * G, D, ROWS), BF), vm((HK * G, D, ROWS), BF),
+            vm((HK * G, 2 * D, ROWS), BF), vm((HK * G, D, ROWS), BF),
             vm((D, SPAN), BF),
             vm((2, D, W), BF), vm((2, D, W), BF),
+            vm((2, W, BLK), BF),
             vm((BLK, ROWS), F32),
             vm((2, D, SPAN), F32),
             vm((HK, 2, SPAN, D), BF),
             vm((HK, 2, HALF, D), BF),
-            vm((HK, 2, HALF, D), BF),
-            vm((HK, CHIPS - 1, 2, SHARD, D), BF),
+            vm((HK, 2, CHIPS - 1, SHARD, D), BF),
             dma((9,)), dma((HK, 2, 2)),
-            dma((HK, 2)), dma((HK, 2)), dma((HK, 2)), dma((HK, 2)), dma((HK,)), dma((HK,)), dma((HK,)), dma((HK,)),
+            dma((HK, 2)), dma((HK, 2)), dma((HK, 2)), dma((HK, 2)),
+            dma((HK, 2)), dma((HK, 2)), dma((HK, 2)), dma((HK, 2)),
         ],
         compiler_params=pltpu.CompilerParams(
             collective_id=0, has_side_effects=True, vmem_limit_bytes=56 * 2**20

time: 52.8 us -> 48.9 us (0.926)
  Pallas kernels: 51.2 us -> 47.4 us
    pallas_call x1, Pallas kernels: 49.6 us -> 45.8 us  [shards(): pl.pallas_call(kernel, out_shape=(vm((ROWS, HK * G * D), BF), vm((ROWS, w...]
where the time goes in v3:
time: 48.9 us; the launch traced here: 48.8 us
  Pallas kernels  47.4 us (97%)
  between operations  1.45 us (3%)
    pallas_call x1, Pallas kernels, shards(): pl.pallas_call(kernel, out_shape=(vm((ROWS, HK * G * D), BF), vm((ROWS, w...  45.8 us
    pallas_call x1, Pallas kernels, shards(): pl.pallas_call(publish, out_shape=tuple((jax.ShapeDtypeStruct(o.shape, o....  1.56 us

profile of v3, /device:TPU:1, one launch (start us, length us, event | category | flops | bytes accessed | tf_op | source)
XLA Modules:
  0.0 48.8 jit_solution(7567620667941945528)
XLA Ops:
  1.3 45.8 %shard_map.110 = (bf16[256,4096]{1,0:T(8,128)(2,1)S(1)}, bf16[256,512]{1,0:T(8,128)(2,1)S(1)}, bf16[256,512]{1,0:T(8,128)(2,1)S(1)}, bf16[64,512]{1,0:T(8,128)(2,1)S(1)}, bf16[64,512]{1,0:T(8,128)(2,1)S(1)}) custom-call(bf16[256,4096]{1,0:T(8,128)(2,1)} %q_hbm.1, bf16[256,4096]{1,0:T(8,128)(2,1)} %g_hbm.1, bf16[256,512]{1,0:T(8,128)(2,1)} %kr_hbm.1, ...), custom_call_target="tpu_custom_call" | custom-call | tf_op jit(solution)/shard_map/pallas_call | solution.py:357
  47.1 1.6 %shard_map.111 = (bf16[256,4096]{1,0:T(8,128)(2,1)}, bf16[256,512]{1,0:T(8,128)(2,1)}, bf16[256,512]{1,0:T(8,128)(2,1)}, bf16[64,512]{1,0:T(8,128)(2,1)}, bf16[64,512]{1,0:T(8,128)(2,1)}) custom-call(bf16[256,4096]{1,0:T(8,128)(2,1)S(1)} %get-tuple-element.10.refs_0_, bf16[256,512]{1,0:T(8,128)(2,1)S(1)} %get-tuple-element.11.refs_1_, ...), custom_call_target="tpu_custom_call" | custom-call | tf_op jit(solution)/shard_map/pallas_call | solution.py:393

commit v4 on v3

--- a/solution.py
+++ b/solution.py
@@ -262,20 +262,20 @@
         f(h, 0)
 
     half = HK * G // 8
+    sends(1, 0)
+    sends(1, 1)
     lax.fori_loop(0, half, prep_four, 0)
     relay(0, 0)
-    sends(1, 0)
-    sends(1, 1)
+    sends(2, 0)
+    sends(2, 1)
     lax.fori_loop(half, 2 * half, prep_four, 0)
     relay(0, 1)
+    sends(3, 0)
+    sends(3, 1)
     relayed(0, 0)
     step(0, 0, b=False, c=False)
-    sends(2, 0)
-    sends(2, 1)
     relayed(0, 1)
     step(1, 1, c=False)
-    sends(3, 0)
-    sends(3, 1)
 
     def four(z, _):
         t = 4 * z + 2

time: 48.9 us -> 48.7 us (level)
  no operation moved by 1% of the time
where the time goes in v4:
time: 48.7 us; the launch traced here: 48.6 us
  Pallas kernels  47.2 us (97%)
  between operations  1.45 us (3%)
    pallas_call x1, Pallas kernels, shards(): pl.pallas_call(kernel, out_shape=(vm((ROWS, HK * G * D), BF), vm((ROWS, w...  45.6 us
    pallas_call x1, Pallas kernels, shards(): pl.pallas_call(publish, out_shape=tuple((jax.ShapeDtypeStruct(o.shape, o....  1.56 us

profile of v4, /device:TPU:1, one launch (start us, length us, event | category | flops | bytes accessed | tf_op | source)
XLA Modules:
  0.0 48.6 jit_solution(12971620439839282446)
XLA Ops:
  1.3 45.6 %shard_map.110 = (bf16[256,4096]{1,0:T(8,128)(2,1)S(1)}, bf16[256,512]{1,0:T(8,128)(2,1)S(1)}, bf16[256,512]{1,0:T(8,128)(2,1)S(1)}, bf16[64,512]{1,0:T(8,128)(2,1)S(1)}, bf16[64,512]{1,0:T(8,128)(2,1)S(1)}) custom-call(bf16[256,4096]{1,0:T(8,128)(2,1)} %q_hbm.1, bf16[256,4096]{1,0:T(8,128)(2,1)} %g_hbm.1, bf16[256,512]{1,0:T(8,128)(2,1)} %kr_hbm.1, ...), custom_call_target="tpu_custom_call" | custom-call | tf_op jit(solution)/shard_map/pallas_call | solution.py:357
  46.9 1.6 %shard_map.111 = (bf16[256,4096]{1,0:T(8,128)(2,1)}, bf16[256,512]{1,0:T(8,128)(2,1)}, bf16[256,512]{1,0:T(8,128)(2,1)}, bf16[64,512]{1,0:T(8,128)(2,1)}, bf16[64,512]{1,0:T(8,128)(2,1)}) custom-call(bf16[256,4096]{1,0:T(8,128)(2,1)S(1)} %get-tuple-element.10.refs_0_, bf16[256,512]{1,0:T(8,128)(2,1)S(1)} %get-tuple-element.11.refs_1_, ...), custom_call_target="tpu_custom_call" | custom-call | tf_op jit(solution)/shard_map/pallas_call | solution.py:393
